TPU v7x, 32 devices: a whole 2x2x4 slice. The times are simulated.
32 devices in a mesh: grp: 2 (over x), seq: 16 (over z, y, core).
Axes of the slice: x: 2, y: 2, z: 4, core: 2. Of those that a mesh axis runs over, the one named last changes fastest.
Arguments:
- tile_embeds: bfloat16 [16384, 1536], P(('grp', 'seq')), parts along dimension 0, may hold values from -6 to 6
- tile_pos: int32 [16384], P(('grp', 'seq')), parts along dimension 0, may hold values from 0 to 4095, as said below
- tile_count: int32 [32], P(('grp', 'seq')), parts along dimension 0, may hold values from 0 to 512, as said below
- slide_weight: bfloat16 [1536, 1536], replicated, may hold values from -0.15625 to 0.15625
- slide_bias: float32 [1536], replicated, may hold values from -3 to 3
- norm_gain: float32 [1536], replicated, may hold values from 0.5 to 1.5
- in_weight: bfloat16 [1536, 3328], replicated, may hold values from -0.15625 to 0.15625
- dt_weight: bfloat16 [1536, 24], replicated, may hold values from -0.15625 to 0.15625
- conv_weight: float32 [2, 4, 1792], replicated, may hold values from -0.6 to 0.6
- conv_bias: float32 [2, 1792], replicated, may hold values from -0.5 to 0.1
- dt_bias: float32 [2, 24], replicated, may hold values from -10.5 to -4
- a_log: float32 [2, 24], replicated, may hold values from 0 to 1.5
- out_gain: float32 [1536], replicated, may hold values from 0.5 to 1.5
- out_weight: bfloat16 [1536, 1536], replicated, may hold values from -0.15625 to 0.15625
Outputs:
- hidden: bfloat16 [8192, 1536], P(('grp', 'seq')), parts along dimension 0
There are 2 independent parts, one for each index of `grp`. A program takes and returns all parts, laid end to end along the dimension named above; an argument that names none is the same for every part. Nothing has to cross between parts.
Inputs may be any that keep to these rules, and one draw needn't show every extreme that they name: The live slots of all readers together hold every slide position exactly once; the position's owner is tile_pos // 256. A reader with live slots holds the same number for every owner, at most 32, and 32 is reached in every draw. Slots beyond a reader's count hold arbitrary positions. `tile_count`: A quarter of the readers hold 512 live tiles, half of them 256, the rest none; which readers is drawn.
All inputs are finite; a program needn't handle non-finite values.
Results may differ from a plain program's by a relative error of at most 0.009.
Values may be sent and summed in bfloat16 or wider, within the bound.
A program may use at most 192 MiB of HBM per device.

v0:
```python
import jax
import jax.numpy as jnp
from jax import lax
from jax.sharding import PartitionSpec as P

HEAD_DIM = 64
NS = 128
KERNEL = 4
HEADS = 24
epsilon = 1e-05
bf16 = jnp.bfloat16
f32 = jnp.float32
precise = lax.Precision.HIGHEST


def dot(a, b):
    return jnp.dot(a, b, preferred_element_type=f32)


def rms_scale(values, scale_gain):
    mean_sq = jnp.mean(values * values, axis=-1, keepdims=True)
    return values * lax.rsqrt(mean_sq + epsilon) * scale_gain


def route(tile_embeds, tile_pos, tile_count, devices, rows):
    slots, width = tile_embeds.shape
    capacity = slots // devices
    index = jnp.arange(slots, dtype=jnp.int32)
    is_live = index < tile_count[0]
    owners = jnp.where(is_live, tile_pos // rows, devices)
    one_hot = owners[:, None] == jnp.arange(devices, dtype=jnp.int32)[None, :]
    below = (index[:, None] >= index[None, :]).astype(bf16)
    counts = dot(below, one_hot.astype(bf16))
    ranking = jnp.sum(jnp.where(one_hot, counts, 0.0), axis=1).astype(jnp.int32) - 1
    target = jnp.where(is_live, owners * capacity + ranking, -1)
    perm = (target[None, :] == index[:, None]).astype(bf16)
    row_tag = jnp.broadcast_to((tile_pos % rows + 1).astype(bf16)[:, None], (slots, 128))
    send = dot(perm, jnp.concatenate([tile_embeds, row_tag], axis=1)).astype(bf16)
    send = send.reshape(devices, capacity, width + 128)
    arrived = lax.all_to_all(send, "seq", split_axis=0, concat_axis=0, tiled=True)
    arrived = arrived.reshape(slots, width + 128)
    tag = arrived[:, width].astype(f32)
    pick = (tag[None, :] == (jnp.arange(rows) + 1).astype(f32)[:, None]).astype(bf16)
    return dot(pick, arrived[:, :width]).astype(bf16)


def neighbours(conv_input, devices):
    up = [(i, i + 1) for i in range(devices - 1)]
    down = [(i + 1, i) for i in range(devices - 1)]
    before = lax.ppermute(conv_input[-(KERNEL - 1):], "seq", up)
    after = lax.ppermute(conv_input[: KERNEL - 1], "seq", down)
    return jnp.concatenate([before, conv_input, after], axis=0).astype(f32)


def per_device(tile_embeds, tile_pos, tile_count, slide_weight, slide_bias, norm_gain, in_weight,
               dt_weight, conv_weight, conv_bias, dt_bias, a_log, out_gain, out_weight):
    devices = lax.axis_size("seq")
    me = lax.axis_index("seq")
    rows = tile_embeds.shape[0] // 2
    e = out_weight.shape[0]
    tiles = route(tile_embeds, tile_pos, tile_count, devices, rows)
    embedded = (dot(tiles, slide_weight) + slide_bias).astype(bf16)
    normed = rms_scale(embedded.astype(f32), norm_gain).astype(bf16)
    projected = dot(normed, in_weight).astype(bf16)
    dt_raw = dot(normed, dt_weight)
    conv_input = projected[:, e:]
    padded = neighbours(conv_input, devices)
    t = jnp.arange(rows)
    lower = t[:, None] >= t[None, :]
    parts = []
    for direction in range(2):
        summed = conv_bias[direction]
        for offset in range(KERNEL):
            first = offset if direction == 0 else 2 * (KERNEL - 1) - offset
            summed = summed + conv_weight[direction, offset] * padded[first:first + rows]
        activated = jax.nn.silu(summed)
        step = jax.nn.softplus(dt_raw + dt_bias[direction])
        log_step = step * -jnp.exp(a_log[direction])
        reach = lower if direction == 0 else lower.T
        log_decay = jnp.dot(reach.astype(f32), log_step, precision=precise)
        total = jnp.sum(log_step, axis=0)
        scaled = (activated[:, :e].reshape(rows, HEADS, HEAD_DIM) * step[:, :, None])
        tail = (scaled * jnp.exp(total[None] - log_decay)[:, :, None]).astype(bf16).reshape(rows, e)
        write = activated[:, e:e + NS].astype(bf16)
        read = activated[:, e + NS:].astype(bf16)
        own = lax.dot_general(write, tail, (((0,), (0,)), ((), ())), preferred_element_type=f32)
        parts.append((scaled.astype(bf16), write, read, log_decay, total, own, reach))
    own = jnp.stack([p[5] for p in parts]).astype(bf16)
    totals = jnp.stack([p[4] for p in parts])
    all_own = lax.all_gather(own, "seq")
    all_totals = lax.all_gather(totals, "seq")
    place = jnp.arange(devices)
    out = jnp.zeros((rows, e), f32)
    for direction in range(2):
        scaled, write, read, log_decay, total, _, reach = parts[direction]
        if direction == 0:
            sums = lax.cumsum(all_totals[:, 0], axis=0)
            gaps = sums[jnp.maximum(me - 1, 0)][None] - sums
            used = place < me
        else:
            sums = lax.cumsum(all_totals[:, 1], axis=0, reverse=True)
            gaps = sums[jnp.minimum(me + 1, devices - 1)][None] - sums
            used = place > me
        weights = jnp.where(used[:, None], jnp.exp(jnp.where(used[:, None], gaps, 0.0)), 0.0)
        weights = jnp.repeat(weights, HEAD_DIM, axis=1)
        incoming = jnp.sum(weights[:, None, :] * all_own[:, direction].astype(f32), axis=0)
        scores = lax.dot_general(read, write, (((1,), (1,)), ((), ())), preferred_element_type=f32)
        turned = log_decay.T
        gap = jnp.where(reach[None], turned[:, :, None] - turned[:, None, :], -1e30)
        mixing = (jnp.exp(gap) * scores[None]).astype(bf16)
        within = jnp.einsum("hts,shp->thp", mixing, scaled, preferred_element_type=f32)
        carried = dot(read, incoming.astype(bf16)) * jnp.repeat(jnp.exp(log_decay), HEAD_DIM, axis=1)
        out = out + within.reshape(rows, e) + carried
    gated = out * jax.nn.silu(projected[:, :e].astype(f32))
    mixed = rms_scale(gated, out_gain).astype(bf16)
    return (embedded.astype(f32) + dot(mixed, out_weight)).astype(bf16)


def solution(mesh):
    return jax.shard_map(
        per_device,
        mesh=mesh,
        in_specs=(P(("grp", "seq"), None), P(("grp", "seq")), P(("grp", "seq"))) + (P(),) * 11,
        out_specs=P(("grp", "seq"), None),
        check_vma=False,
    )
```

profile of v0, /device:TPU:0, one launch (start us, length us, event | category | flops | bytes accessed | tf_op | source)
XLA Modules:
  0.0 216.4 jit_solution(809983163653743281)
XLA Ops:
  8.3 3.7 %convolution_convert_fusion.1 = bf16[512,1664]{1,0:T(8,128)(2,1)} fusion(bf16[512,128]{1,0:T(8,128)(2,1)S(1)} %broadcast_in_dim.108, bf16[512,1536]{1,0:T(8,128)(2,1)} %param.14, s32[512]{0:T(512)S(1)} %add_select_fusion.2), kind=kOutput, calls=%fused_computation.21 | convolution fusion | flops 876937216 | bytes 3409920 | tf_op jit(solution)/shard_map/dot_general | solution.py:17
  12.1 7.5 %all-to-all-start = ((bf16[16,32,1664]{2,1,0:T(8,128)(2,1)}), bf16[16,32,1664]{2,1,0:T(8,128)(2,1)S(1)}, u32[]{:S(2)}, u32[]{:S(2)}) async-start(bf16[16,32,1664]{2,1,0:T(8,128)(2,1)} %bitcast.1), calls=%async_computation | async-start | bytes 3407872 | tf_op jit(solution)/shard_map/all_to_all | solution.py:40
  20.0 33.9 %all-to-all-done = bf16[16,32,1664]{2,1,0:T(8,128)(2,1)S(1)} async-done(((bf16[16,32,1664]{2,1,0:T(8,128)(2,1)}), bf16[16,32,1664]{2,1,0:T(8,128)(2,1)S(1)}, u32[]{:S(2)}, u32[]{:S(2)}) %all-to-all-start) | async-done | bytes 1703968 | tf_op jit(solution)/shard_map/all_to_all | solution.py:40
  54.0 4.3 %multiply_reduce_fusion.1 = (f32[256]{0:T(256)S(1)}, f32[256,1536]{1,0:T(8,128)S(1)}) fusion(f32[1536]{0:T(1024)S(1)} %copy-done.26, bf16[1536,1536]{1,0:T(8,128)(2,1)} %param.17, bf16[512,1664]{1,0:T(8,128)(2,1)S(1)} %bitcast.66, f32[512]{0:T(512)S(1)} %convert_reduce_fusion, f32[256]{0:T(256)S(1)} %add_convert_fusion), kind=kOutput, calls=%fused_computation.70 | convolution fusion | flops 1613102848 | bytes 7876608 | tf_op jit(solution)/shard_map/dot_general | solution.py:17
  58.3 7.3 %convolution_convert_fusion = bf16[256,3328]{1,0:T(8,128)(2,1)S(1)} fusion(bf16[1536,3328]{1,0:T(8,128)(2,1)} %param.20, f32[256,1536]{1,0:T(8,128)S(1)} %get-tuple-element.44, f32[1536]{0:T(1024)S(1)} %copy-done.18, f32[256]{0:T(256)S(1)} %add_rsqrt_fusion.1), kind=kOutput, calls=%fused_computation.8 | convolution fusion | flops 2619277312 | bytes 13507584 | tf_op jit(solution)/shard_map/dot_general | solution.py:17
  66.4 3.3 %collective-permute-start = (bf16[3,1792]{1,0:T(4,128)(2,1)}, bf16[3,1792]{1,0:T(4,128)(2,1)}, u32[]{:S(2)}, u32[]{:S(2)}) collective-permute-start(bf16[3,1792]{1,0:T(4,128)(2,1)} %get-tuple-element.27), channel_id=1, source_target_pairs={{0,1},{1,2},{2,3},{3,4},{4,5},{5,6},{6,7},{7,8},{8,9},{9,10},{10,1... | collective-permute-start | bytes 32264 | tf_op jit(solution)/shard_map/ppermute | solution.py:50
  72.4 1.5 fusion.84
  75.6 1.6 copy.47
  77.4 1.6 copy.50
  79.1 1.6 copy.49
  82.1 2.4 %fusion.81 = (bf16[256,1792]{1,0:T(8,128)(2,1)S(1)}, f32[256,1792]{1,0:T(8,128)S(1)}, bf16[256,1792]{1,0:T(8,128)(2,1)S(1)}, f32[256,1792]{1,0:T(8,128)S(1)}) fusion(f32[262,1792]{1,0:T(8,128)S(1)} %maximum_convert_fusion, f32[1792]{0:T(1024)S(1)} %get-tuple-element.10, f32[1792]{0:T(1024)S(1)} %get-tuple-element.11, f32[1792]{0:T(1024)S(1)} %get-tuple-element.12, ...), kind=kLoop, calls=%fused_computation.157 | loop fusion | flops 11927552 | bytes 18421760 | tf_op jit(solution)/shard_map/convert.10
  90.6 26.8 %all-gather.1 = f32[16,2,24]{2,1,0:T(2,128)S(1)} all-gather(f32[1,2,24]{2,1,0:T(2,128)S(1)} %maximum_bitcast_fusion), channel_id=2, replica_groups=mesh['grp'=2,'seq'=16] {'seq'}, dimensions={0}, use_global_device_ids=true | all-gather | bytes 3264 | tf_op jit(solution)/shard_map/all_gather | solution.py:91
  119.6 1.6 copy.51
  122.0 1.6 copy.55
  123.7 2.7 %slice.164 = f32[256,1536]{1,0:T(8,128)} slice(f32[256,1792]{1,0:T(8,128)} %copy-done.2), slice={[0:256], [0:1536]} | slice | bytes 3145728 | tf_op jit(solution)/shard_map/slice | solution.py:82
  126.6 1.9 copy.46
  129.5 3.8 %fusion.2 = f32[24,64,256]{2,1,0:T(8,128)} fusion(f32[256,256]{1,0:T(8,128)S(1)} %fusion.62, f32[24,256]{1,0:T(8,128)} %bitcast.78, pred[256,256]{1,0:T(8,128)(4,1)} %iota_compare_fusion.5, f32[256,24,64]{0,2,1:T(8,128)S(1)} %bitcast.67, f32[256,24]{0,1:T(8,128)S(1)} %get-tuple-element.18), kind=kOutput, calls=%fused_computation.9 | convolution fusion | flops 208404480 | bytes 3522560 | tf_op jit(solution)/shard_map/hts,shp->thp/dot_general | solution.py:111
  133.3 3.1 %copy.52 = f32[256,1536]{1,0:T(8,128)} copy(f32[256,1536]{0,1:T(8,128)} %bitcast.69) | data formatting | bytes 3145728 | tf_op jit(solution)/shard_map/reshape | solution.py:113
  138.0 2.5 %fusion.3 = f32[24,64,256]{2,1,0:T(8,128)S(1)} fusion(f32[256,256]{1,0:T(8,128)S(1)} %fusion.57, f32[24,256]{1,0:T(8,128)S(1)} %bitcast.77, pred[256,256]{1,0:T(8,128)(4,1)} %iota_compare_fusion.4, f32[256,24,64]{0,2,1:T(8,128)S(1)} %bitcast.68, f32[256,24]{0,1:T(8,128)S(1)} %get-tuple-element.34), kind=kOutput, calls=%fused_computation.10 | convolution fusion | flops 208404480 | bytes 3522560 | tf_op jit(solution)/shard_map/hts,shp->thp/dot_general | solution.py:111
  140.5 1.6 copy.54
  142.1 54.5 %all-gather.4.cloned.1.call-done = bf16[16,2,128,1536]{3,2,1,0:T(8,128)(2,1)} async-done(((bf16[1,2,128,1536]{3,2,1,0:T(8,128)(2,1)}), bf16[16,2,128,1536]{3,2,1,0:T(8,128)(2,1)}) %all-gather.4.cloned.1.call-update) | async-done | bytes 12582928 | tf_op jit(solution)/shard_map/all_gather | solution.py:90
  196.6 6.6 %fusion = (bf16[128,1536]{1,0:T(8,128)(2,1)S(1)}, bf16[128,1536]{1,0:T(8,128)(2,1)S(1)}) fusion(bf16[16,2,128,1536]{3,2,1,0:T(8,128)(2,1)} %all-gather.4.cloned.1.call-done, f32[16,1536]{1,0:T(8,128)S(1)} %mul.309, f32[16,1536]{1,0:T(8,128)S(1)} %copy-done.15), kind=kLoop, calls=%fused_computation.1 | loop fusion | flops 18481152 | bytes 13565952 | tf_op jit(solution)/shard_map/reduce_sum | solution.py:106
  204.8 2.3 %multiply_reduce_fusion = (f32[256]{0:T(256)S(1)}, f32[256,1536]{1,0:T(8,128)S(1)}) fusion(bf16[256,3328]{1,0:T(8,128)(2,1)} %copy-done.14, f32[256,1536]{1,0:T(8,128)S(1)} %fusion.17, f32[256,1536]{1,0:T(8,128)S(1)} %copy-done.9, bf16[128,1536]{1,0:T(8,128)(2,1)S(1)} %get-tuple-element.5, bf16[256,1792]{1,0:T(8,128)(2,1)} %copy-done.13), kind=kOutput, calls=%fused_computation.64 | convolution fusion | flops 104595200 | bytes 5964800 | tf_op jit(solution)/shard_map/dot_general | solution.py:17
  207.2 2.4 %fusion.20 = bf16[256,1536]{1,0:T(8,128)(2,1)} fusion(f32[256,1536]{1,0:T(8,128)S(1)} %copy-done.11, bf16[1536,1536]{1,0:T(8,128)(2,1)S(1)} %bitcast.76, f32[256,1536]{1,0:T(8,128)S(1)} %get-tuple-element.48, f32[1536]{0:T(1024)S(1)} %copy-done.27, f32[256]{0:T(256)S(1)} %add_rsqrt_fusion), kind=kOutput, calls=%fused_computation.32 | convolution fusion | flops 1209925632 | bytes 8657920 | tf_op jit(solution)/shard_map/dot_general | solution.py:17
  (115 shorter events, 21.4 us)
Async XLA Ops:
  6.5 64.4 %copy-start = (bf16[1536,24]{0,1:T(8,128)(2,1)S(1)}, bf16[1536,24]{0,1:T(8,128)(2,1)}, u32[]{:S(2)}) copy-start(bf16[1536,24]{0,1:T(8,128)(2,1)} %param.21) | copy-start | bytes 221188
  12.1 7.6 %copy-start.17 = (f32[2,1792]{1,0:T(2,128)S(1)}, f32[2,1792]{1,0:T(2,128)}, u32[]{:S(2)}) copy-start(f32[2,1792]{1,0:T(2,128)} %param.23) | copy-start | bytes 43012
  12.1 7.7 %copy-start.16 = (f32[2,4,1792]{2,1,0:T(4,128)S(1)}, f32[2,4,1792]{2,1,0:T(4,128)}, u32[]{:S(2)}) copy-start(f32[2,4,1792]{2,1,0:T(4,128)} %param.22) | copy-start | bytes 172036
  12.1 7.8 %copy-start.24 = (f32[2,24]{1,0:T(2,128)S(1)}, f32[2,24]{1,0:T(2,128)}, u32[]{:S(2)}) copy-start(f32[2,24]{1,0:T(2,128)} %param.25) | copy-start | bytes 580
  12.1 7.9 %copy-start.25 = (f32[2,24]{1,0:T(2,128)S(1)}, f32[2,24]{1,0:T(2,128)}, u32[]{:S(2)}) copy-start(f32[2,24]{1,0:T(2,128)} %param.24) | copy-start | bytes 580
  12.1 41.9 %copy-start.26 = (f32[1536]{0:T(1024)S(1)}, f32[1536]{0:T(1024)}, u32[]{:S(2)}) copy-start(f32[1536]{0:T(1024)} %param.18) | copy-start | bytes 18436
  12.1 41.8 %all-to-all-start = ((bf16[16,32,1664]{2,1,0:T(8,128)(2,1)}), bf16[16,32,1664]{2,1,0:T(8,128)(2,1)S(1)}, u32[]{:S(2)}, u32[]{:S(2)}) async-start(bf16[16,32,1664]{2,1,0:T(8,128)(2,1)} %bitcast.1), calls=%async_computation | async-start | bytes 3407872 | tf_op jit(solution)/shard_map/all_to_all | solution.py:40
  19.6 177.0 %all-gather.4.cloned.1.call-start = ((), (), s32[]{:S(2)}) async-start(), calls=%async_computation.1 | async-start | bytes 13369344 | tf_op jit(solution)/shard_map/all_gather | solution.py:90
  20.0 51.0 %copy-start.23 = (f32[24]{0:T(128)}, f32[24]{0:T(128)S(1)}, u32[]{:S(2)}) copy-start(f32[24]{0:T(128)S(1)} %get-tuple-element.42) | copy-start | bytes 292
  54.0 4.3 %copy-start.18 = (f32[1536]{0:T(1024)S(1)}, f32[1536]{0:T(1024)}, u32[]{:S(2)}) copy-start(f32[1536]{0:T(1024)} %param.19) | copy-start | bytes 18436
  58.3 12.6 %copy-start.10 = (f32[256,1536]{1,0:T(8,128)}, f32[256,1536]{1,0:T(8,128)S(1)}, u32[]{:S(2)}) copy-start(f32[256,1536]{1,0:T(8,128)S(1)} %get-tuple-element.44) | copy-start | bytes 4718596
  65.7 9.2 %copy-start.14 = (bf16[256,3328]{1,0:T(8,128)(2,1)}, bf16[256,3328]{1,0:T(8,128)(2,1)S(1)}, u32[]{:S(2)}) copy-start(bf16[256,3328]{1,0:T(8,128)(2,1)S(1)} %convolution_convert_fusion) | copy-start | bytes 5111812
  66.4 14.4 %collective-permute-start = (bf16[3,1792]{1,0:T(4,128)(2,1)}, bf16[3,1792]{1,0:T(4,128)(2,1)}, u32[]{:S(2)}, u32[]{:S(2)}) collective-permute-start(bf16[3,1792]{1,0:T(4,128)(2,1)} %get-tuple-element.27), channel_id=1, source_target_pairs={{0,1},{1,2},{2,3},{3,4},{4,5},{5,6},{6,7},{7,8},{8,9},{9,10},{10,1... | collective-permute-start | bytes 32264 | tf_op jit(solution)/shard_map/ppermute | solution.py:50
  69.6 11.1 %collective-permute-start.1 = (bf16[3,1792]{1,0:T(4,128)(2,1)S(1)}, bf16[3,1792]{1,0:T(4,128)(2,1)}, u32[]{:S(2)}, u32[]{:S(2)}) collective-permute-start(bf16[3,1792]{1,0:T(4,128)(2,1)S(1)} %get-tuple-element.28), channel_id=1, source_target_pairs={{1,0},{2,1},{3,2},{4,3},{5,4},{6,5},{7,6},{8,7},{9,8},{10,9},{11,1... | collective-permute-start | bytes 32264 | tf_op jit(solution)/shard_map/ppermute | solution.py:51
  71.5 3.5 %copy-start.19 = (f32[24]{0:T(128)}, f32[24]{0:T(128)S(1)}, u32[]{:S(2)}) copy-start(f32[24]{0:T(128)S(1)} %get-tuple-element.17) | copy-start | bytes 292
  71.5 3.5 %copy-start.21 = (f32[24]{0:T(128)}, f32[24]{0:T(128)S(1)}, u32[]{:S(2)}) copy-start(f32[24]{0:T(128)S(1)} %get-tuple-element.33) | copy-start | bytes 292
  82.1 2.5 %copy-start.4 = (f32[256,1536]{1,0:T(8,128)S(1)}, f32[256,1536]{1,0:T(8,128)}, u32[]{:S(2)}) copy-start(f32[256,1536]{1,0:T(8,128)} %copy.47) | copy-start | bytes 4718596
  84.6 2.6 %copy-start.5 = (f32[256,1536]{1,0:T(8,128)S(1)}, f32[256,1536]{1,0:T(8,128)}, u32[]{:S(2)}) copy-start(f32[256,1536]{1,0:T(8,128)} %copy.50) | copy-start | bytes 4718596
  84.6 3.2 %copy-start.6 = (f32[256,1536]{1,0:T(8,128)S(1)}, f32[256,1536]{1,0:T(8,128)}, u32[]{:S(2)}) copy-start(f32[256,1536]{1,0:T(8,128)} %copy.49) | copy-start | bytes 4718596
  140.4 56.2 %copy-start.15 = (f32[16,1536]{1,0:T(8,128)S(1)}, f32[16,1536]{1,0:T(8,128)}, u32[]{:S(2)}) copy-start(f32[16,1536]{1,0:T(8,128)} %mul.278) | copy-start | bytes 294916
  142.1 61.2 %copy-start.3 = (f32[256,1536]{1,0:T(8,128)S(1)}, f32[256,1536]{1,0:T(8,128)}, u32[]{:S(2)}) copy-start(f32[256,1536]{1,0:T(8,128)} %copy.51) | copy-start | bytes 4718596
  142.1 61.2 %copy-start.7 = (f32[256,1536]{1,0:T(8,128)S(1)}, f32[256,1536]{1,0:T(8,128)}, u32[]{:S(2)}) copy-start(f32[256,1536]{1,0:T(8,128)} %copy.52) | copy-start | bytes 4718596
  196.6 6.7 %copy-start.8 = (f32[256,1536]{1,0:T(8,128)S(1)}, f32[256,1536]{1,0:T(8,128)}, u32[]{:S(2)}) copy-start(f32[256,1536]{1,0:T(8,128)} %copy.54) | copy-start | bytes 4718596
  203.3 3.8 %slice-start = ((s8[4718592]{0:T(1024)(128)(4,1)}), s8[4194304]{0:T(1024)(128)(4,1)S(1)}, s32[]{:S(2)}) async-start(s8[4718592]{0:T(1024)(128)(4,1)} %bitcast.75), calls=%async_computation.2 | async-start | bytes 8388608
  (11 other events, 21.7 us)
Sparse Core Ops, SparseCore 0:
  89.4 107.1 all-gather.3
where the time goes:
time: 217 us; the launch traced here: 216 us
  waiting for transfers between devices  88.4 us (41%)
  matrix products  34 us (16%)
  blocking collectives  26.8 us (12%)
  local copies, waits for them, and re-layouts  26.6 us (12%)
  between operations  14.7 us (7%)
  other arithmetic  13.8 us (6%)
  starting transfers between devices  12.1 us (6%)
    all_gather x1, waiting for transfers between devices, per_device(): all_own = lax.all_gather(own, 'seq')  54.5 us
    all_to_all x1, waiting for transfers between devices, route(): lax.all_to_all(send, 'seq', split_axis=0, concat_axis=0, tiled=True)  33.9 us
    all_gather x1, blocking collectives, per_device(): all_totals = lax.all_gather(totals, 'seq')  26.8 us
    dot_general x8, matrix products, dot(): return jnp.dot(a, b, preferred_element_type=f32)  22.3 us
    all_to_all x1, starting transfers between devices, route(): lax.all_to_all(send, 'seq', split_axis=0, concat_axis=0, tiled=True)  7.53 us
    reduce_sum x1, other arithmetic, per_device(): jnp.sum(weights[:, None, :] * all_own[:, direction].astype(f32), axis=0)  6.64 us
    dot_general x2, matrix products, per_device(): jnp.einsum('hts,shp->thp', mixing, scaled, preferred_element_type=f32)  6.29 us
    slice x4, local copies, waits for them, and re-layouts, per_device(): scaled = activated[:, :e].reshape(rows, HEADS, HEAD_DIM) * step[:, :, None]  5.23 us
  transfers between devices with their start and end apart: 4, of which 2 were waited for; matrix products, arithmetic and copies ran while one was open for 17% of the time, Pallas kernels for 0%

commit v1 on v0

v1 whole, which is shorter than its diff:
```python
import functools

import jax
import jax.numpy as jnp
from jax import lax
from jax.experimental import pallas as pl
from jax.experimental.pallas import tpu as pltpu
from jax.sharding import PartitionSpec as P

HEAD_DIM = 64
NS = 128
KERNEL = 4
HEADS = 24
GROUP = 4
epsilon = 1e-05
bf16 = jnp.bfloat16
f32 = jnp.float32
precise = lax.Precision.HIGHEST


def dot(a, b):
    return jnp.dot(a, b, preferred_element_type=f32)


def rms_scale(values, scale_gain):
    mean_sq = jnp.mean(values * values, axis=-1, keepdims=True)
    return values * lax.rsqrt(mean_sq + epsilon) * scale_gain


def route(tile_embeds, tile_pos, tile_count, devices, rows):
    slots, width = tile_embeds.shape
    capacity = slots // devices
    index = jnp.arange(slots, dtype=jnp.int32)
    is_live = index < tile_count[0]
    owners = jnp.where(is_live, tile_pos // rows, devices)
    one_hot = owners[:, None] == jnp.arange(devices, dtype=jnp.int32)[None, :]
    below = (index[:, None] >= index[None, :]).astype(bf16)
    counts = dot(below, one_hot.astype(bf16))
    ranking = jnp.sum(jnp.where(one_hot, counts, 0.0), axis=1).astype(jnp.int32) - 1
    target = jnp.where(is_live, owners * capacity + ranking, -1)
    perm = (target[None, :] == index[:, None]).astype(bf16)
    row_tag = jnp.broadcast_to((tile_pos % rows + 1).astype(bf16)[:, None], (slots, 128))
    send = dot(perm, jnp.concatenate([tile_embeds, row_tag], axis=1)).astype(bf16)
    send = send.reshape(devices, capacity, width + 128)
    arrived = lax.all_to_all(send, "seq", split_axis=0, concat_axis=0, tiled=True)
    arrived = arrived.reshape(slots, width + 128)
    tag = arrived[:, width].astype(f32)
    pick = (tag[None, :] == (jnp.arange(rows) + 1).astype(f32)[:, None]).astype(bf16)
    return dot(pick, arrived[:, :width]).astype(bf16)


def exact_dot(a, b):
    return jnp.dot(a, b, precision=precise, preferred_element_type=f32)


def mixer_kernel(n, cin_ref, gate_ref, dt_ref, conv_w_ref, conv_b_ref, dt_b_ref, a_log_ref, expand_ref, gain_ref,
                 mixed_ref, pad, halo, tots, totx, log_x, log_t, step_x, scaled, tail, write, read, acc, score,
                 sbuf, r1, tbuf, r2, pbuf, r3, halo_sem, tot_send, tot_recv, sem1s, sem1r, sem2s, sem2r, sem3s, sem3r):
    rows, e = gate_ref.shape
    wide = cin_ref.shape[1]
    planes = n // GROUP
    part = e // GROUP
    me = lax.axis_index("seq")
    plane, q = me // GROUP, me % GROUP
    halo_width = halo.shape[1]

    def remote(src, dst, send, recv, to):
        return pltpu.make_async_remote_copy(src_ref=src, dst_ref=dst, send_sem=send, recv_sem=recv,
                                            device_id={"seq": to}, device_id_type=pl.DeviceIdType.MESH)

    barrier = pltpu.get_barrier_semaphore()
    for k in range(1, n):
        pl.semaphore_signal(barrier, inc=1, device_id={"seq": (me + k) % n}, device_id_type=pl.DeviceIdType.MESH)
    pl.semaphore_wait(barrier, n - 1)

    halos = [
        remote(cin_ref.at[pl.ds(rows - halo_width, halo_width)], halo.at[0], halo_sem.at[0], halo_sem.at[2], (me + 1) % n),
        remote(cin_ref.at[pl.ds(0, halo_width)], halo.at[1], halo_sem.at[1], halo_sem.at[3], (me + n - 1) % n),
    ]
    for copy in halos:
        copy.start()

    t_at = lax.broadcasted_iota(jnp.int32, (rows, rows), 0)
    s_at = lax.broadcasted_iota(jnp.int32, (rows, rows), 1)
    steps = []
    for d in range(2):
        x = dt_ref[...] + dt_b_ref[d:d + 1, :]
        step = jnp.maximum(x, 0.0) + jnp.log1p(jnp.exp(-jnp.abs(x)))
        log_step = step * -jnp.exp(a_log_ref[d:d + 1, :])
        steps.append((step, log_step))
    own_tots = jnp.concatenate(
        [jnp.sum(steps[0][1], axis=0, keepdims=True), jnp.sum(steps[1][1], axis=0, keepdims=True),
         jnp.zeros((6, 128), f32)], axis=0)
    tots[me] = own_tots
    tot_copies = []
    for k in range(1, n):
        to = (me + k) % n
        copy = remote(tots.at[me], tots.at[me], tot_send.at[k], tot_recv.at[k], to)
        copy.start()
        tot_copies.append(copy)
    for d in range(2):
        step, log_step = steps[d]
        reach = (t_at >= s_at) if d == 0 else (t_at <= s_at)
        log_decay = exact_dot(reach.astype(f32), log_step)
        log_t[d] = log_decay.T
        log_x[d] = exact_dot(log_decay, expand_ref[...])
        step_x[d] = exact_dot(step, expand_ref[...])

    for copy in halos:
        copy.wait()

    def fill(c, carry):
        cols = pl.ds(pl.multiple_of(c * 128, 128), 128)
        pad[pl.ds(halo_width, rows), cols] = cin_ref[:, cols].astype(f32)
        pad[pl.ds(0, halo_width), cols] = jnp.where(me > 0, halo[0, :, cols].astype(f32), 0.0)
        pad[pl.ds(halo_width + rows, halo_width), cols] = jnp.where(me < n - 1, halo[1, :, cols].astype(f32), 0.0)
        return carry

    lax.fori_loop(0, wide // 128, fill, 0)

    def activated(d, cols):
        summed = conv_b_ref[d:d + 1, cols]
        for j in range(KERNEL):
            shift = j - (KERNEL - 1) if d == 0 else (KERNEL - 1) - j
            taps = conv_w_ref[d * KERNEL + j:d * KERNEL + j + 1, cols]
            summed = summed + taps * pad[pl.ds(halo_width + shift, rows), cols]
        return summed * jax.nn.sigmoid(summed)

    for d in range(2):
        write[d] = activated(d, slice(e, e + NS)).astype(bf16)
        read[d] = activated(d, slice(e + NS, e + 2 * NS)).astype(bf16)

    def signals(c, carry):
        cols = pl.ds(pl.multiple_of(c * 128, 128), 128)
        for d in range(2):
            value = activated(d, cols) * step_x[d, :, cols]
            scaled[pl.ds(d * rows, rows), cols] = value.astype(bf16)
            decay = log_x[d, :, cols]
            last = decay[rows - 1:rows] if d == 0 else decay[0:1]
            tail[d, :, cols] = (value * jnp.exp(last - decay)).astype(bf16)
        return carry

    lax.fori_loop(0, e // 128, signals, 0)

    for d in range(2):
        write_t = write[d].astype(f32).T.astype(bf16)
        for p in range(GROUP):
            sbuf[p, d] = dot(write_t, tail[d, :, p * part:(p + 1) * part]).astype(bf16)
    first = []
    for k in range(1, GROUP):
        other = (q + k) % GROUP
        copy = remote(sbuf.at[other], r1.at[q], sem1s.at[k], sem1r.at[k], plane * GROUP + other)
        copy.start()
        first.append(copy)
    r1[q] = sbuf[q]

    for d in range(2):
        reach = (t_at >= s_at) if d == 0 else (t_at <= s_at)
        product = lax.dot_general(read[d], write[d], (((1,), (1,)), ((), ())), preferred_element_type=f32)
        score[d] = jnp.where(reach, product, 0.0)

    def within(pair, carry):
        cols = pl.ds(pl.multiple_of(pair * 128, 128), 128)
        lower = t_at >= s_at
        pair_signal = scaled[:, cols]
        halves = []
        for i in range(2):
            lane = i * HEAD_DIM
            column = jnp.where(lower, log_x[0, :, cols][:, lane:lane + 1], log_x[1, :, cols][:, lane:lane + 1])
            line = jnp.where(lower, log_t[0, pl.ds(pair * 2 + i, 1), :], log_t[1, pl.ds(pair * 2 + i, 1), :])
            weights = jnp.exp(column - line)
            mixing = jnp.concatenate([(weights * score[0]).astype(bf16), (weights * score[1]).astype(bf16)], axis=1)
            halves.append(dot(mixing, pair_signal))
        lanes = lax.broadcasted_iota(jnp.int32, (rows, 128), 1)
        acc[:, cols] = jnp.where(lanes < HEAD_DIM, halves[0], halves[1])
        return carry

    pairs = e // 128
    lax.fori_loop(0, pairs // 2, within, 0)

    for copy in tot_copies:
        copy.wait()
    totx[...] = exact_dot(tots[...].reshape(n * 8, 128), expand_ref[...])
    mine = pl.ds(pl.multiple_of(q * part, 128), part)

    def decay_of(device, d):
        return jnp.exp(totx[pl.ds(device * 8, 8), mine][d:d + 1])

    def plane_decay(z, d):
        logs = totx[pl.ds(z * GROUP * 8, GROUP * 8), mine]
        return jnp.exp(sum(logs[8 * j + d:8 * j + d + 1] for j in range(GROUP)))

    for copy in first:
        copy.wait()
    for d in range(2):
        order = range(GROUP) if d == 0 else range(GROUP - 1, -1, -1)
        state = jnp.zeros((NS, part), f32)
        for j in order:
            state = state * decay_of(plane * GROUP + j, d) + r1[j, d].astype(f32)
        tbuf[d] = state.astype(bf16)
    second = []
    for k in range(1, planes):
        z = (plane + k) % planes
        copy = remote(tbuf.at[jnp.where(z > plane, 0, 1)], r2.at[plane], sem2s.at[k], sem2r.at[k], z * GROUP + q)
        copy.start()
        second.append(copy)
    r2[plane] = jnp.zeros((NS, part), bf16)

    lax.fori_loop(pairs // 2, pairs, within, 0)

    for copy in second:
        copy.wait()
    for d in range(2):
        state = jnp.zeros((NS, part), f32)
        for z in (range(planes) if d == 0 else range(planes - 1, -1, -1)):
            reached = z < plane if d == 0 else z > plane
            state = jnp.where(reached, state * plane_decay(z, d) + r2[z].astype(f32), state)
        for j in (range(GROUP) if d == 0 else range(GROUP - 1, -1, -1)):
            pbuf[j, d] = state.astype(bf16)
            state = state * decay_of(plane * GROUP + j, d) + r1[j, d].astype(f32)
    third = []
    for k in range(1, GROUP):
        other = (q + k) % GROUP
        copy = remote(pbuf.at[other], r3.at[q], sem3s.at[k], sem3r.at[k], plane * GROUP + other)
        copy.start()
        third.append(copy)
    r3[q] = pbuf[q]
    for copy in third:
        copy.wait()

    def finish(c, squares):
        for i in range(part // 128):
            cols = pl.ds(pl.multiple_of(c * part + i * 128, 128), 128)
            total = acc[:, cols]
            for d in range(2):
                total = total + dot(read[d], r3[c, d, :, i * 128:(i + 1) * 128]) * jnp.exp(log_x[d, :, cols])
            gate = gate_ref[:, cols].astype(f32)
            gated = total * (gate * jax.nn.sigmoid(gate))
            acc[:, cols] = gated
            squares = squares + gated * gated
        return squares

    squares = lax.fori_loop(0, GROUP, finish, jnp.zeros((rows, 128), f32))
    inverse = lax.rsqrt(jnp.sum(squares, axis=1, keepdims=True) / e + epsilon)

    def emit(c, carry):
        cols = pl.ds(pl.multiple_of(c * 128, 128), 128)
        mixed_ref[:, cols] = (acc[:, cols] * inverse * gain_ref[:, cols]).astype(bf16)
        return carry

    lax.fori_loop(0, e // 128, emit, 0)


def mixer(devices, cin, gate, dt_raw, conv_weight, conv_bias, dt_bias, a_log, out_gain):
    rows, e = gate.shape
    wide = cin.shape[1]
    part = e // GROUP
    planes = devices // GROUP
    pad_heads = ((0, 0), (0, 128 - HEADS))
    expand = (jnp.arange(128)[:, None] == (jnp.arange(e) // HEAD_DIM)[None, :]).astype(f32)
    dma = pltpu.SemaphoreType.DMA
    vmem = pltpu.VMEM
    return pl.pallas_call(
        functools.partial(mixer_kernel, devices),
        out_shape=jax.ShapeDtypeStruct((rows, e), bf16),
        in_specs=[pl.BlockSpec(memory_space=pltpu.VMEM)] * 9,
        out_specs=pl.BlockSpec(memory_space=pltpu.VMEM),
        scratch_shapes=[
            vmem((rows + 32, wide), f32), vmem((2, 16, wide), bf16), vmem((devices, 8, 128), f32),
            vmem((devices * 8, e), f32), vmem((2, rows, e), f32), vmem((2, 128, rows), f32),
            vmem((2, rows, e), f32), vmem((2 * rows, e), bf16), vmem((2, rows, e), bf16),
            vmem((2, rows, NS), bf16), vmem((2, rows, NS), bf16), vmem((rows, e), f32), vmem((2, rows, rows), f32),
            vmem((GROUP, 2, NS, part), bf16), vmem((GROUP, 2, NS, part), bf16), vmem((2, NS, part), bf16),
            vmem((planes, NS, part), bf16), vmem((GROUP, 2, NS, part), bf16), vmem((GROUP, 2, NS, part), bf16),
            dma((4,)), dma((devices,)), dma((devices,)), dma((GROUP,)), dma((GROUP,)), dma((planes,)), dma((planes,)),
            dma((GROUP,)), dma((GROUP,)),
        ],
        compiler_params=pltpu.CompilerParams(collective_id=0, has_side_effects=True, vmem_limit_bytes=50 * 2**20),
        cost_estimate=pl.CostEstimate(flops=2 * 10**9, bytes_accessed=4 * 10**6, transcendentals=4 * 10**6),
    )(cin, gate, dt_raw, conv_weight.reshape(2 * KERNEL, wide), conv_bias, jnp.pad(dt_bias, pad_heads),
      jnp.pad(a_log, pad_heads), expand, out_gain[None])


def per_device(tile_embeds, tile_pos, tile_count, slide_weight, slide_bias, norm_gain, in_weight,
               dt_weight, conv_weight, conv_bias, dt_bias, a_log, out_gain, out_weight):
    devices = lax.axis_size("seq")
    rows = tile_embeds.shape[0] // 2
    e = out_weight.shape[0]
    tiles = route(tile_embeds, tile_pos, tile_count, devices, rows)
    embedded = (dot(tiles, slide_weight) + slide_bias).astype(bf16)
    normed = rms_scale(embedded.astype(f32), norm_gain).astype(bf16)
    cin = dot(normed, in_weight[:, e:]).astype(bf16)
    gate = dot(normed, in_weight[:, :e]).astype(bf16)
    dt_raw = dot(normed, jnp.pad(dt_weight, ((0, 0), (0, 128 - HEADS))))
    mixed = mixer(devices, cin, gate, dt_raw, conv_weight, conv_bias, dt_bias, a_log, out_gain)
    return (embedded.astype(f32) + dot(mixed, out_weight)).astype(bf16)


def solution(mesh):
    return jax.shard_map(
        per_device,
        mesh=mesh,
        in_specs=(P(("grp", "seq"), None), P(("grp", "seq")), P(("grp", "seq"))) + (P(),) * 11,
        out_specs=P(("grp", "seq"), None),
        check_vma=False,
    )
```

time: 217 us -> 116 us (0.53)
  waiting for transfers between devices: 88.4 us -> 34 us
  Pallas kernels: 0 us -> 49.7 us
  blocking collectives: 26.8 us -> 0 us
  local copies, waits for them, and re-layouts: 26.6 us -> 0.23 us
  matrix products: 34 us -> 20 us
  between operations: 14.7 us -> 0.92 us
  other arithmetic: 13.8 us -> 2.52 us
  starting transfers between devices: 12.1 us -> 7.53 us
    all_gather x1 -> x0, waiting for transfers between devices: 54.5 us -> none  [per_device(): all_own = lax.all_gather(own, 'seq')]
    pallas_call x0 -> x1, Pallas kernels: none -> 49.7 us  [mixer(): pl.pallas_call(functools.partial(mixer_kernel, devices), out_shape=jax.Sh...]
    all_gather x1 -> x0, blocking collectives: 26.8 us -> none  [per_device(): all_totals = lax.all_gather(totals, 'seq')]
    dot_general x8 -> x0, matrix products: 11.7 us -> none  [the longest x2 6.29 us: per_device(): jnp.einsum('hts,shp->thp', mixing, scaled, preferred_element_type=f32)]
    reshape x4 -> x1, local copies, waits for them, and re-layouts: 7.97 us -> 0.02 us  [mixer(): conv_weight.reshape(2 * KERNEL, wide)]
    slice x9 -> x0, local copies, waits for them, and re-layouts: 7.1 us -> none  [the longest x4 5.23 us: per_device(): scaled = activated[:, :e].reshape(rows, HEADS, HEAD_DIM) * step[:, :, None]]
    reduce_sum x1 -> x0, other arithmetic: 6.64 us -> none  [per_device(): jnp.sum(weights[:, None, :] * all_own[:, direction].astype(f32), axis=0)]
    mul x10 -> x0, local copies, waits for them, and re-layouts: 6.63 us -> none  [the longest x4 3.46 us: per_device(): scaled = activated[:, :e].reshape(rows, HEADS, HEAD_DIM) * step[:, :, None]]
  transfers between devices with their start and end apart: 4 -> 1, of which waited for: 2 -> 1; matrix products, arithmetic and copies ran while one was open for 17% -> 0% of each run, Pallas kernels for 0% -> 0%
where the time goes in v1:
time: 116 us; the launch traced here: 115 us
  Pallas kernels  49.7 us (43%)
  waiting for transfers between devices  34 us (29%)
  matrix products  20 us (17%)
  starting transfers between devices  7.53 us (6%)
  other arithmetic  2.52 us (2%)
    pallas_call x1, Pallas kernels, mixer(): pl.pallas_call(functools.partial(mixer_kernel, devices), out_shape=jax.Sh...  49.7 us
    all_to_all x1, waiting for transfers between devices, route(): lax.all_to_all(send, 'seq', split_axis=0, concat_axis=0, tiled=True)  34 us
    dot_general x7, matrix products, dot(): return jnp.dot(a, b, preferred_element_type=f32)  20 us
    all_to_all x1, starting transfers between devices, route(): lax.all_to_all(send, 'seq', split_axis=0, concat_axis=0, tiled=True)  7.53 us
  transfers between devices with their start and end apart: 1, of which 1 were waited for; matrix products, arithmetic and copies ran while one was open for 0% of the time, Pallas kernels for 0%

profile of v1, /device:TPU:0, one launch (start us, length us, event | category | flops | bytes accessed | tf_op | source)
XLA Modules:
  0.0 115.0 jit_solution(13146151985593843731)
XLA Ops:
  0.7 0.7 fusion.34
  1.3 0.3 fusion.17
  1.6 0.1 broadcast_in_dim.15
  1.8 3.8 %convolution_convert_fusion = bf16[512,1664]{1,0:T(8,128)(2,1)} fusion(bf16[512,128]{1,0:T(8,128)(2,1)S(1)} %broadcast_in_dim.15, bf16[512,1536]{1,0:T(8,128)(2,1)} %param.14, s32[512]{0:T(512)S(1)} %add_select_fusion.3), kind=kOutput, calls=%fused_computation.4 | convolution fusion | flops 876937216 | bytes 3409920 | tf_op jit(solution)/shard_map/dot_general | solution.py:22
  5.5 0.0 copy-start.8
  5.6 7.5 %all-to-all-start = ((bf16[16,32,1664]{2,1,0:T(8,128)(2,1)}), bf16[16,32,1664]{2,1,0:T(8,128)(2,1)S(1)}, u32[]{:S(2)}, u32[]{:S(2)}) async-start(bf16[16,32,1664]{2,1,0:T(8,128)(2,1)} %bitcast.13), calls=%async_computation | async-start | bytes 3407872 | tf_op jit(solution)/shard_map/all_to_all | solution.py:45
  13.1 0.0 copy-done.5
  13.1 0.0 copy-done.6
  13.1 0.0 copy-done.4
  13.2 0.1 fusion.20.expand_ref
  13.3 34.0 %all-to-all-done = bf16[16,32,1664]{2,1,0:T(8,128)(2,1)S(1)} async-done(((bf16[16,32,1664]{2,1,0:T(8,128)(2,1)}), bf16[16,32,1664]{2,1,0:T(8,128)(2,1)S(1)}, u32[]{:S(2)}, u32[]{:S(2)}) %all-to-all-start) | async-done | bytes 1703968 | tf_op jit(solution)/shard_map/all_to_all | solution.py:45
  47.4 0.1 convert_reduce_fusion
  47.5 0.0 copy-start.3
  47.5 5.3 %multiply_reduce_fusion = (f32[256]{0:T(256)S(1)}, f32[256,1536]{1,0:T(8,128)}) fusion(f32[1536]{0:T(1024)S(1)} %copy-done.8, bf16[1536,1536]{1,0:T(8,128)(2,1)} %param.17, bf16[512,1664]{1,0:T(8,128)(2,1)S(1)} %bitcast.12, f32[512]{0:T(512)S(1)} %convert_reduce_fusion, f32[256]{0:T(256)S(1)} %add_convert_fusion), kind=kOutput, calls=%fused_computation.18 | convolution fusion | flops 1613102848 | bytes 7876608 | tf_op jit(solution)/shard_map/dot_general | solution.py:22
  52.8 1.6 %multiply_convert_fusion = bf16[256,1536]{1,0:T(8,128)(2,1)S(1)} fusion(f32[256,1536]{1,0:T(8,128)} %get-tuple-element.8, f32[1536]{0:T(1024)S(1)} %copy-done.3, f32[256]{0:T(256)S(1)} %add_rsqrt_fusion), kind=kLoop, calls=%fused_computation.17 | loop fusion | flops 1179648 | bytes 2366464 | tf_op jit(solution)/shard_map/convert_element_type | solution.py:291
  54.5 0.0 slice-start
  54.5 3.9 %fusion.7.gate_ref = bf16[256,1536]{1,0:T(8,128)(2,1)S(1)} fusion(bf16[256,1536]{1,0:T(8,128)(2,1)S(1)} %multiply_convert_fusion, bf16[1536,3328]{1,0:T(8,128)(2,1)} %param.20), kind=kOutput, calls=%fused_computation.11 | convolution fusion | flops 1208352768 | bytes 6291456 | tf_op jit(solution)/shard_map/dot_general | solution.py:22
  58.4 0.0 copy-start.7
  58.4 0.0 copy-start
  58.4 0.0 slice-start.1
  58.4 4.2 %fusion.10.cin_ref = bf16[256,1792]{1,0:T(8,128)(2,1)S(1)} fusion(bf16[256,1536]{1,0:T(8,128)(2,1)S(1)} %multiply_convert_fusion, bf16[1536,3328]{1,0:T(8,128)(2,1)} %param.20), kind=kOutput, calls=%fused_computation.12 | convolution fusion | flops 1409744896 | bytes 7208960 | tf_op jit(solution)/shard_map/dot_general | solution.py:22
  62.6 0.3 fusion.24.dt_ref
  63.0 49.7 %shard_map.136 = bf16[256,1536]{1,0:T(8,128)(2,1)S(1)} custom-call(bf16[256,1792]{1,0:T(8,128)(2,1)S(1)} %fusion.10.cin_ref, bf16[256,1536]{1,0:T(8,128)(2,1)S(1)} %fusion.7.gate_ref, f32[256,128]{1,0:T(8,128)S(1)} %fusion.24.dt_ref, f32[8,1792]{1,0:T(8,128)S(1)} %reshape.49.conv_w_ref, f32[2,1792]{1,0:T(2,128)S(1)} %copy-done, f32[2,128]{1,0:T(2,128)S(1)} %pad.12.dt_b_ref, ...), custom_call_target="tpu_custom_call" | custom-call | flops 2000000000 | bytes 4000000 | tf_op jit(solution)/shard_map/pallas_call | solution.py:263
  112.8 2.3 %fusion.6 = bf16[256,1536]{1,0:T(8,128)(2,1)} fusion(f32[256,1536]{1,0:T(8,128)S(1)} %copy-done.1, bf16[256,1536]{1,0:T(8,128)(2,1)S(1)} %shard_map.136, bf16[1536,1536]{1,0:T(8,128)(2,1)S(1)} %bitcast.15), kind=kOutput, calls=%fused_computation.9 | convolution fusion | flops 1208745984 | bytes 7864320 | tf_op jit(solution)/shard_map/dot_general | solution.py:22
  (22 shorter events, 0.1 us)
Async XLA Ops:
  5.5 7.6 %copy-start.5 = (f32[2,24]{1,0:T(2,128)S(1)}, f32[2,24]{1,0:T(2,128)}, u32[]{:S(2)}) copy-start(f32[2,24]{1,0:T(2,128)} %param.24) | copy-start | bytes 580
  5.5 7.6 %copy-start.6 = (f32[2,24]{1,0:T(2,128)S(1)}, f32[2,24]{1,0:T(2,128)}, u32[]{:S(2)}) copy-start(f32[2,24]{1,0:T(2,128)} %param.25) | copy-start | bytes 580
  5.5 7.6 %copy-start.4 = (f32[1536]{0:T(1024)S(1)}, f32[1536]{0:T(1024)}, u32[]{:S(2)}) copy-start(f32[1536]{0:T(1024)} %param.26) | copy-start | bytes 18436
  5.5 7.6 %copy-start.2 = (f32[2,4,1792]{2,1,0:T(4,128)S(1)}, f32[2,4,1792]{2,1,0:T(4,128)}, u32[]{:S(2)}) copy-start(f32[2,4,1792]{2,1,0:T(4,128)} %param.22) | copy-start | bytes 172036
  5.5 41.9 %copy-start.8 = (f32[1536]{0:T(1024)S(1)}, f32[1536]{0:T(1024)}, u32[]{:S(2)}) copy-start(f32[1536]{0:T(1024)} %param.18) | copy-start | bytes 18436
  5.6 41.8 %all-to-all-start = ((bf16[16,32,1664]{2,1,0:T(8,128)(2,1)}), bf16[16,32,1664]{2,1,0:T(8,128)(2,1)S(1)}, u32[]{:S(2)}, u32[]{:S(2)}) async-start(bf16[16,32,1664]{2,1,0:T(8,128)(2,1)} %bitcast.13), calls=%async_computation | async-start | bytes 3407872 | tf_op jit(solution)/shard_map/all_to_all | solution.py:45
  47.5 5.4 %copy-start.3 = (f32[1536]{0:T(1024)S(1)}, f32[1536]{0:T(1024)}, u32[]{:S(2)}) copy-start(f32[1536]{0:T(1024)} %param.19) | copy-start | bytes 18436
  54.5 58.3 %slice-start = ((s8[4718592]{0:T(1024)(128)(4,1)}), s8[4194304]{0:T(1024)(128)(4,1)S(1)}, s32[]{:S(2)}) async-start(s8[4718592]{0:T(1024)(128)(4,1)} %bitcast.14), calls=%async_computation.1 | async-start | bytes 8388608
  58.4 4.3 %copy-start.7 = (bf16[1536,24]{0,1:T(8,128)(2,1)S(1)}, bf16[1536,24]{0,1:T(8,128)(2,1)}, u32[]{:S(2)}) copy-start(bf16[1536,24]{0,1:T(8,128)(2,1)} %param.21) | copy-start | bytes 221188
  58.4 4.6 %copy-start = (f32[2,1792]{1,0:T(2,128)S(1)}, f32[2,1792]{1,0:T(2,128)}, u32[]{:S(2)}) copy-start(f32[2,1792]{1,0:T(2,128)} %conv_b_ref.1) | copy-start | bytes 43012
  58.4 54.4 %slice-start.1 = ((s8[4718592]{0:T(1024)(128)(4,1)}), s8[524288]{0:T(1024)(128)(4,1)S(1)}, s32[]{:S(2)}) async-start(s8[4718592]{0:T(1024)(128)(4,1)} %bitcast.14), calls=%async_computation.2 | async-start | bytes 1048576
  63.0 49.8 %copy-start.1 = (f32[256,1536]{1,0:T(8,128)S(1)}, f32[256,1536]{1,0:T(8,128)}, u32[]{:S(2)}) copy-start(f32[256,1536]{1,0:T(8,128)} %get-tuple-element.8) | copy-start | bytes 4718596

commit v2 on v1

v2 whole, which is shorter than its diff:
```python
import functools

import jax
import jax.numpy as jnp
from jax import lax
from jax.experimental import pallas as pl
from jax.experimental.pallas import tpu as pltpu
from jax.sharding import PartitionSpec as P

HEAD_DIM = 64
NS = 128
KERNEL = 4
HEADS = 24
GROUP = 4
LOAD = 384
epsilon = 1e-05
bf16 = jnp.bfloat16
f32 = jnp.float32
precise = lax.Precision.HIGHEST


def dot(a, b):
    return jnp.dot(a, b, preferred_element_type=f32)


def rms_scale(values, scale_gain):
    mean_sq = jnp.mean(values * values, axis=-1, keepdims=True)
    return values * lax.rsqrt(mean_sq + epsilon) * scale_gain


def plan(tile_pos, tile_count, devices, rows):
    slots = tile_pos.shape[0]
    capacity = slots // devices
    index = jnp.arange(slots, dtype=jnp.int32)
    is_live = index < tile_count[0]
    owners = jnp.where(is_live, tile_pos // rows, devices)
    one_hot = owners[:, None] == jnp.arange(devices, dtype=jnp.int32)[None, :]
    below = (index[:, None] >= index[None, :]).astype(bf16)
    counts = dot(below, one_hot.astype(bf16))
    ranking = jnp.sum(jnp.where(one_hot, counts, 0.0), axis=1).astype(jnp.int32) - 1
    target = jnp.where(is_live, owners * capacity + ranking, -1)
    row_tag = (tile_pos % rows + 1).astype(f32)
    sent = jnp.sum(jnp.where(target[None, :] == index[:, None], row_tag[None, :], 0.0), axis=1)
    share = 128 // capacity
    spread = jnp.tile(sent.reshape(devices, capacity), (1, share))
    place = jnp.arange(128) // capacity == lax.axis_index("seq") % share
    tags = jnp.where(place[None], spread, 0.0)
    return target[None], jnp.broadcast_to(tags[:, None, :], (devices, 8, 128))


def exact_dot(a, b):
    return jnp.dot(a, b, precision=precise, preferred_element_type=f32)


def mixer_kernel(n, tiles_ref, target_ref, tags_ref, slide_w_ref, slide_b_ref, norm_ref, in_w_ref, dt_w_ref,
                 conv_w_ref, conv_b_ref, dt_b_ref, a_log_ref, expand_ref, gain_ref, mixed_ref, embedded_ref,
                 slide_w, in_w, out_rows, in_rows, in_tags, normed, gate_ref, cin_ref, dt_ref,
                 weight_sem, tag_send, tag_recv, row_send, row_recv, pad, halo, tots, totx, log_x, log_t, step_x, scaled, tail, write, read, acc, score,
                 sbuf, r1, tbuf, r2, pbuf, r3, halo_sem, tot_send, tot_recv, sem1s, sem1r, sem2s, sem2r, sem3s, sem3r):
    rows, e = gate_ref.shape
    wide = cin_ref.shape[1]
    planes = n // GROUP
    part = e // GROUP
    me = lax.axis_index("seq")
    plane, q = me // GROUP, me % GROUP
    halo_width = halo.shape[1]

    def remote(src, dst, send, recv, to):
        return pltpu.make_async_remote_copy(src_ref=src, dst_ref=dst, send_sem=send, recv_sem=recv,
                                            device_id={"seq": to}, device_id_type=pl.DeviceIdType.MESH)

    barrier = pltpu.get_barrier_semaphore()
    for k in range(1, n):
        pl.semaphore_signal(barrier, inc=1, device_id={"seq": (me + k) % n}, device_id_type=pl.DeviceIdType.MESH)
    weight_copies = [pltpu.make_async_copy(slide_w_ref, slide_w, weight_sem.at[0]),
                     pltpu.make_async_copy(in_w_ref, in_w, weight_sem.at[1])]
    for copy in weight_copies:
        copy.start()
    slots = tiles_ref.shape[0]
    capacity = slots // n
    order = lax.broadcasted_iota(jnp.int32, (slots, slots), 0)
    perm = jnp.where(order == target_ref[...], 1.0, 0.0).astype(bf16)
    out_rows[0] = dot(perm, tiles_ref[:, :LOAD]).astype(bf16)
    pl.semaphore_wait(barrier, n - 1)

    def tag_copy(k):
        to = (me + k) % n
        return remote(tags_ref.at[to], in_tags.at[me], tag_send.at[k], tag_recv.at[k], to)

    def row_copy(c, k):
        to = (me + k) % n
        return remote(out_rows.at[c, pl.ds(pl.multiple_of(to * capacity, capacity), capacity)],
                      in_rows.at[c, pl.ds(pl.multiple_of(me * capacity, capacity), capacity)],
                      row_send.at[c, k], row_recv.at[c, k], to)

    def start_tag(k, carry):
        tag_copy(k).start()
        return carry

    def wait_tag(k, carry):
        tag_copy(k).wait()
        return carry

    loads = e // LOAD
    for c in range(loads):
        if c > 0:
            out_rows[c] = dot(perm, tiles_ref[:, c * LOAD:(c + 1) * LOAD]).astype(bf16)

        def start_row(k, carry, c=c):
            row_copy(c, k).start()
            return carry

        lax.fori_loop(1, n, start_row, 0)
        if c == 0:
            lax.fori_loop(1, n, start_tag, 0)
    in_tags[me] = tags_ref[me]
    kept = pl.ds(pl.multiple_of(me * capacity, capacity), capacity)
    for c in range(loads):
        in_rows[c, kept, :] = out_rows[c, kept, :]
    lax.fori_loop(1, n, wait_tag, 0)
    share = 128 // capacity
    row_at = (lax.broadcasted_iota(jnp.int32, (rows, 128), 0) + 1).astype(f32)
    picks = []
    for g in range(slots // 128):
        line = sum(in_tags[g * share + j, 0:1, :] for j in range(share))
        picks.append(jnp.where(row_at == line, 1.0, 0.0).astype(bf16))
    pick = jnp.concatenate(picks, axis=1)
    weight_copies[0].wait()
    for c in range(loads):

        def wait_row(k, carry, c=c):
            row_copy(c, k).wait()
            return carry

        lax.fori_loop(1, n, wait_row, 0)
        placed = dot(pick, in_rows[c]).astype(bf16)
        for w in range(e // 512):
            cols = slice(w * 512, (w + 1) * 512)
            product = dot(placed, slide_w[c * LOAD:(c + 1) * LOAD, cols])
            acc[:, cols] = product if c == 0 else acc[:, cols] + product

    def embed(c, squares):
        cols = pl.ds(pl.multiple_of(c * 128, 128), 128)
        value = (acc[:, cols] + slide_b_ref[:, cols]).astype(bf16)
        embedded_ref[:, cols] = value
        value = value.astype(f32)
        return squares + value * value

    squares = lax.fori_loop(0, e // 128, embed, jnp.zeros((rows, 128), f32))
    inverse = lax.rsqrt(jnp.sum(squares, axis=1, keepdims=True) / e + epsilon)

    def norm(c, carry):
        cols = pl.ds(pl.multiple_of(c * 128, 128), 128)
        normed[:, cols] = (embedded_ref[:, cols].astype(f32) * inverse * norm_ref[:, cols]).astype(bf16)
        return carry

    lax.fori_loop(0, e // 128, norm, 0)
    dt_ref[...] = dot(normed[...], dt_w_ref[...])
    weight_copies[1].wait()

    def project_cin(c, carry):
        from_cols = pl.ds(pl.multiple_of(e + c * 256, 256), 256)
        cin_ref[:, pl.ds(pl.multiple_of(c * 256, 256), 256)] = dot(normed[...], in_w[:, from_cols]).astype(bf16)
        return carry

    def project_gate(c, carry):
        cols = pl.ds(pl.multiple_of(c * 256, 256), 256)
        gate_ref[:, cols] = dot(normed[...], in_w[:, cols]).astype(bf16)
        return carry

    lax.fori_loop(0, wide // 256, project_cin, 0)

    halos = [
        remote(cin_ref.at[pl.ds(rows - halo_width, halo_width)], halo.at[0], halo_sem.at[0], halo_sem.at[2], (me + 1) % n),
        remote(cin_ref.at[pl.ds(0, halo_width)], halo.at[1], halo_sem.at[1], halo_sem.at[3], (me + n - 1) % n),
    ]
    for copy in halos:
        copy.start()

    t_at = lax.broadcasted_iota(jnp.int32, (rows, rows), 0)
    s_at = lax.broadcasted_iota(jnp.int32, (rows, rows), 1)
    steps = []
    for d in range(2):
        x = dt_ref[...] + dt_b_ref[d:d + 1, :]
        step = jnp.maximum(x, 0.0) + jnp.log1p(jnp.exp(-jnp.abs(x)))
        log_step = step * -jnp.exp(a_log_ref[d:d + 1, :])
        steps.append((step, log_step))
    own_tots = jnp.concatenate(
        [jnp.sum(steps[0][1], axis=0, keepdims=True), jnp.sum(steps[1][1], axis=0, keepdims=True),
         jnp.zeros((6, 128), f32)], axis=0)
    tots[me] = own_tots
    tot_copies = []
    for k in range(1, n):
        to = (me + k) % n
        copy = remote(tots.at[me], tots.at[me], tot_send.at[k], tot_recv.at[k], to)
        copy.start()
        tot_copies.append(copy)
    for d in range(2):
        step, log_step = steps[d]
        reach = (t_at >= s_at) if d == 0 else (t_at <= s_at)
        log_decay = exact_dot(reach.astype(f32), log_step)
        log_t[d] = log_decay.T
        log_x[d] = exact_dot(log_decay, expand_ref[...])
        step_x[d] = exact_dot(step, expand_ref[...])

    lax.fori_loop(0, e // 256, project_gate, 0)
    for copy in halos:
        copy.wait()

    def fill(c, carry):
        cols = pl.ds(pl.multiple_of(c * 128, 128), 128)
        pad[pl.ds(halo_width, rows), cols] = cin_ref[:, cols].astype(f32)
        pad[pl.ds(0, halo_width), cols] = jnp.where(me > 0, halo[0, :, cols].astype(f32), 0.0)
        pad[pl.ds(halo_width + rows, halo_width), cols] = jnp.where(me < n - 1, halo[1, :, cols].astype(f32), 0.0)
        return carry

    lax.fori_loop(0, wide // 128, fill, 0)

    def activated(d, cols):
        summed = conv_b_ref[d:d + 1, cols]
        for j in range(KERNEL):
            shift = j - (KERNEL - 1) if d == 0 else (KERNEL - 1) - j
            taps = conv_w_ref[d * KERNEL + j:d * KERNEL + j + 1, cols]
            summed = summed + taps * pad[pl.ds(halo_width + shift, rows), cols]
        return summed * jax.nn.sigmoid(summed)

    for d in range(2):
        write[d] = activated(d, slice(e, e + NS)).astype(bf16)
        read[d] = activated(d, slice(e + NS, e + 2 * NS)).astype(bf16)

    def signals(c, carry):
        cols = pl.ds(pl.multiple_of(c * 128, 128), 128)
        for d in range(2):
            value = activated(d, cols) * step_x[d, :, cols]
            scaled[pl.ds(d * rows, rows), cols] = value.astype(bf16)
            decay = log_x[d, :, cols]
            last = decay[rows - 1:rows] if d == 0 else decay[0:1]
            tail[d, :, cols] = (value * jnp.exp(last - decay)).astype(bf16)
        return carry

    pieces = part // 128
    write_t = [write[d].astype(f32).T.astype(bf16) for d in range(2)]

    def first_copy(i, k):
        other = (q + k) % GROUP
        return remote(sbuf.at[i, other], r1.at[i, q], sem1s.at[i, k], sem1r.at[i, k], plane * GROUP + other)

    def second_copy(i, k):
        z = (plane + k) % planes
        return remote(tbuf.at[i, jnp.where(z > plane, 0, 1)], r2.at[i, plane], sem2s.at[i, k], sem2r.at[i, k],
                      z * GROUP + q)

    def third_copy(i, k):
        other = (q + k) % GROUP
        return remote(pbuf.at[i, other], r3.at[i, q], sem3s.at[i, k], sem3r.at[i, k], plane * GROUP + other)

    for i in range(pieces):
        for p in range(GROUP):
            signals(p * pieces + i, 0)
            at = p * part + i * 128
            for d in range(2):
                sbuf[i, p, d] = dot(write_t[d], tail[d, :, at:at + 128]).astype(bf16)
        for k in range(1, GROUP):
            first_copy(i, k).start()
        r1[i, q] = sbuf[i, q]

    for d in range(2):
        reach = (t_at >= s_at) if d == 0 else (t_at <= s_at)
        product = lax.dot_general(read[d], write[d], (((1,), (1,)), ((), ())), preferred_element_type=f32)
        score[d] = jnp.where(reach, product, 0.0)

    def within(pair, carry):
        cols = pl.ds(pl.multiple_of(pair * 128, 128), 128)
        lower = t_at >= s_at
        pair_signal = scaled[:, cols]
        halves = []
        for i in range(2):
            lane = i * HEAD_DIM
            column = jnp.where(lower, log_x[0, :, cols][:, lane:lane + 1], log_x[1, :, cols][:, lane:lane + 1])
            line = jnp.where(lower, log_t[0, pl.ds(pair * 2 + i, 1), :], log_t[1, pl.ds(pair * 2 + i, 1), :])
            weights = jnp.exp(column - line)
            mixing = jnp.concatenate([(weights * score[0]).astype(bf16), (weights * score[1]).astype(bf16)], axis=1)
            halves.append(dot(mixing, pair_signal))
        lanes = lax.broadcasted_iota(jnp.int32, (rows, 128), 1)
        acc[:, cols] = jnp.where(lanes < HEAD_DIM, halves[0], halves[1])
        return carry

    pairs = e // 128

    for copy in tot_copies:
        copy.wait()
    totx[...] = exact_dot(tots[...].reshape(n * 8, 128), expand_ref[...])
    lax.fori_loop(0, 2, within, 0)

    def lanes_of(i):
        return pl.ds(pl.multiple_of(q * part + i * 128, 128), 128)

    def decay_of(device, d, i):
        return jnp.exp(totx[pl.ds(device * 8, 8), lanes_of(i)][d:d + 1])

    def plane_decay(z, d, i):
        logs = totx[pl.ds(z * GROUP * 8, GROUP * 8), lanes_of(i)]
        return jnp.exp(sum(logs[8 * j + d:8 * j + d + 1] for j in range(GROUP)))

    for i in range(pieces):
        for k in range(1, GROUP):
            first_copy(i, k).wait()
        for d in range(2):
            state = jnp.zeros((NS, 128), f32)
            for j in (range(GROUP) if d == 0 else range(GROUP - 1, -1, -1)):
                state = state * decay_of(plane * GROUP + j, d, i) + r1[i, j, d].astype(f32)
            tbuf[i, d] = state.astype(bf16)
        for k in range(1, planes):
            second_copy(i, k).start()
        r2[i, plane] = jnp.zeros((NS, 128), bf16)
        lax.fori_loop(2 + i, 3 + i, within, 0)

    for i in range(pieces):
        for k in range(1, planes):
            second_copy(i, k).wait()
        for d in range(2):
            state = jnp.zeros((NS, 128), f32)
            for z in (range(planes) if d == 0 else range(planes - 1, -1, -1)):
                reached = z < plane if d == 0 else z > plane
                state = jnp.where(reached, state * plane_decay(z, d, i) + r2[i, z].astype(f32), state)
            for j in (range(GROUP) if d == 0 else range(GROUP - 1, -1, -1)):
                pbuf[i, j, d] = state.astype(bf16)
                state = state * decay_of(plane * GROUP + j, d, i) + r1[i, j, d].astype(f32)
        for k in range(1, GROUP):
            third_copy(i, k).start()
        r3[i, q] = pbuf[i, q]
        lax.fori_loop(2 + pieces + 2 * i, 4 + pieces + 2 * i, within, 0)
    lax.fori_loop(2 + 3 * pieces, pairs, within, 0)
    for i in range(pieces):
        for k in range(1, GROUP):
            third_copy(i, k).wait()

    def finish(c, squares):
        for i in range(part // 128):
            cols = pl.ds(pl.multiple_of(c * part + i * 128, 128), 128)
            total = acc[:, cols]
            for d in range(2):
                total = total + dot(read[d], r3[i, c, d]) * jnp.exp(log_x[d, :, cols])
            gate = gate_ref[:, cols].astype(f32)
            gated = total * (gate * jax.nn.sigmoid(gate))
            acc[:, cols] = gated
            squares = squares + gated * gated
        return squares

    squares = lax.fori_loop(0, GROUP, finish, jnp.zeros((rows, 128), f32))
    inverse = lax.rsqrt(jnp.sum(squares, axis=1, keepdims=True) / e + epsilon)

    def emit(c, carry):
        cols = pl.ds(pl.multiple_of(c * 128, 128), 128)
        mixed_ref[:, cols] = (acc[:, cols] * inverse * gain_ref[:, cols]).astype(bf16)
        return carry

    lax.fori_loop(0, e // 128, emit, 0)


def layer(devices, tile_embeds, target, tags, slide_weight, slide_bias, norm_gain, in_weight, dt_weight,
          conv_weight, conv_bias, dt_bias, a_log, out_gain):
    slots, e = tile_embeds.shape
    rows = slots // 2
    wide = e + 2 * NS
    pieces = e // GROUP // 128
    planes = devices // GROUP
    pad_heads = ((0, 0), (0, 128 - HEADS))
    expand = (jnp.arange(128)[:, None] == (jnp.arange(e) // HEAD_DIM)[None, :]).astype(f32)
    dma = pltpu.SemaphoreType.DMA
    vmem = pltpu.VMEM
    held = pl.BlockSpec(memory_space=pltpu.VMEM)
    far = pl.BlockSpec(memory_space=pl.ANY)
    loads = e // LOAD
    return pl.pallas_call(
        functools.partial(mixer_kernel, devices),
        out_shape=[jax.ShapeDtypeStruct((rows, e), bf16), jax.ShapeDtypeStruct((rows, e), bf16)],
        in_specs=[held, held, held, far, held, held, far] + [held] * 7,
        out_specs=[held, held],
        scratch_shapes=[
            vmem((e, e), bf16), vmem((e, e + wide), bf16), vmem((loads, slots, LOAD), bf16),
            vmem((loads, slots, LOAD), bf16), vmem((devices, 8, 128), f32), vmem((rows, e), bf16),
            vmem((rows, e), bf16), vmem((rows, wide), bf16), vmem((rows, 128), f32),
            dma((2,)), dma((devices,)), dma((devices,)), dma((loads, devices)), dma((loads, devices)),
            vmem((rows + 32, wide), f32), vmem((2, 16, wide), bf16), vmem((devices, 8, 128), f32),
            vmem((devices * 8, e), f32), vmem((2, rows, e), f32), vmem((2, 128, rows), f32),
            vmem((2, rows, e), f32), vmem((2 * rows, e), bf16), vmem((2, rows, e), bf16),
            vmem((2, rows, NS), bf16), vmem((2, rows, NS), bf16), vmem((rows, e), f32), vmem((2, rows, rows), f32),
            vmem((pieces, GROUP, 2, NS, 128), bf16), vmem((pieces, GROUP, 2, NS, 128), bf16),
            vmem((pieces, 2, NS, 128), bf16), vmem((pieces, planes, NS, 128), bf16),
            vmem((pieces, GROUP, 2, NS, 128), bf16), vmem((pieces, GROUP, 2, NS, 128), bf16),
            dma((4,)), dma((devices,)), dma((devices,)), dma((pieces, GROUP)), dma((pieces, GROUP)),
            dma((pieces, planes)), dma((pieces, planes)), dma((pieces, GROUP)), dma((pieces, GROUP)),
        ],
        compiler_params=pltpu.CompilerParams(collective_id=0, has_side_effects=True, vmem_limit_bytes=58 * 2**20),
        cost_estimate=pl.CostEstimate(flops=8 * 10**9, bytes_accessed=18 * 10**6, transcendentals=4 * 10**6),
    )(tile_embeds, target, tags, slide_weight, slide_bias[None], norm_gain[None], in_weight,
      jnp.pad(dt_weight, pad_heads), conv_weight.reshape(2 * KERNEL, wide), conv_bias, jnp.pad(dt_bias, pad_heads),
      jnp.pad(a_log, pad_heads), expand, out_gain[None])


def per_device(tile_embeds, tile_pos, tile_count, slide_weight, slide_bias, norm_gain, in_weight,
               dt_weight, conv_weight, conv_bias, dt_bias, a_log, out_gain, out_weight):
    devices = lax.axis_size("seq")
    rows = tile_embeds.shape[0] // 2
    target, tags = plan(tile_pos, tile_count, devices, rows)
    mixed, embedded = layer(devices, tile_embeds, target, tags, slide_weight, slide_bias, norm_gain, in_weight,
                            dt_weight, conv_weight, conv_bias, dt_bias, a_log, out_gain)
    return (embedded.astype(f32) + dot(mixed, out_weight)).astype(bf16)


def solution(mesh):
    return jax.shard_map(
        per_device,
        mesh=mesh,
        in_specs=(P(("grp", "seq"), None), P(("grp", "seq")), P(("grp", "seq"))) + (P(),) * 11,
        out_specs=P(("grp", "seq"), None),
        check_vma=False,
    )
```

time: 116 us -> 105 us (0.905)
  Pallas kernels: 49.7 us -> 85.6 us
  waiting for transfers between devices: 34 us -> 0 us
  matrix products: 20 us -> 5.32 us
  local copies, waits for them, and re-layouts: 0.23 us -> 10.6 us
  starting transfers between devices: 7.53 us -> 0 us
    pallas_call x1, Pallas kernels: 49.7 us -> 85.6 us  [layer(): pl.pallas_call(functools.partial(mixer_kernel, devices), out_shape=[jax.S...]
    all_to_all x1 -> x0, waiting for transfers between devices: 34 us -> none  [route(): lax.all_to_all(send, 'seq', split_axis=0, concat_axis=0, tiled=True)]
    dot_general x7 -> x2, matrix products: 20 us -> 5.32 us  [dot(): return jnp.dot(a, b, preferred_element_type=f32)]
    all_to_all x1 -> x0, starting transfers between devices: 7.53 us -> none  [route(): lax.all_to_all(send, 'seq', split_axis=0, concat_axis=0, tiled=True)]
    broadcast_in_dim x2 -> x4, local copies, waits for them, and re-layouts: 0.14 us -> 4.51 us  [the longest x1 1.3 us: layer(): slide_bias[None]]
    pad x2 -> x3, local copies, waits for them, and re-layouts: 0.01 us -> 3.31 us  [the longest x1 1.25 us: layer(): jnp.pad(dt_bias, pad_heads)]
    reshape x1, local copies, waits for them, and re-layouts: 0.02 us -> 1.46 us  [layer(): conv_weight.reshape(2 * KERNEL, wide)]
  transfers between devices with their start and end apart: 1 -> 0, of which waited for: 1 -> 0; matrix products, arithmetic and copies ran while one was open for 0% -> 0% of each run, Pallas kernels for 0% -> 0%
where the time goes in v2:
time: 105 us; the launch traced here: 104 us
  Pallas kernels  85.6 us (82%)
  local copies, waits for them, and re-layouts  10.6 us (10%)
  matrix products  5.32 us (5%)
  other arithmetic  1.87 us (2%)
    pallas_call x1, Pallas kernels, layer(): pl.pallas_call(functools.partial(mixer_kernel, devices), out_shape=[jax.S...  85.6 us
    dot_general x2, matrix products, dot(): return jnp.dot(a, b, preferred_element_type=f32)  5.32 us

profile of v2, /device:TPU:0, one launch (start us, length us, event | category | flops | bytes accessed | tf_op | source)
XLA Modules:
  0.0 104.0 jit_solution(12329442889284326016)
XLA Ops:
  0.7 1.2 %pad.12.dt_b_ref = f32[2,128]{1,0:T(2,128)} pad(f32[2,24]{1,0:T(2,128)} %param.24, f32[]{:T(128)} %constant.77.clone.1), padding=0_0x0_104 | pad | bytes 1220 | tf_op jit(solution)/shard_map/jit(_pad)/pad | solution.py:398
  1.9 1.2 %pad.13.a_log_ref = f32[2,128]{1,0:T(2,128)} pad(f32[2,24]{1,0:T(2,128)} %param.25, f32[]{:T(128)} %constant.77.clone.1), padding=0_0x0_104 | pad | bytes 1220 | tf_op jit(solution)/shard_map/jit(_pad)/pad | solution.py:399
  3.2 0.7 fusion.9
  3.9 0.3 fusion.1
  4.1 0.0 copy-start
  4.1 0.2 select_reduce_fusion
  4.3 0.1 tile.10
  4.4 1.3 %broadcast_in_dim.69.slide_b_ref = f32[1,1536]{1,0:T(1,128)} reshape(f32[1536]{0:T(1024)} %param.18) | data formatting | bytes 12288 | tf_op jit(solution)/shard_map/broadcast_in_dim | solution.py:397
  5.7 1.3 %broadcast_in_dim.70.norm_ref = f32[1,1536]{1,0:T(1,128)} reshape(f32[1536]{0:T(1024)} %param.19) | data formatting | bytes 12288 | tf_op jit(solution)/shard_map/broadcast_in_dim | solution.py:397
  7.0 1.3 %broadcast_in_dim.71.gain_ref = f32[1,1536]{1,0:T(1,128)} reshape(f32[1536]{0:T(1024)} %param.26) | data formatting | bytes 12288 | tf_op jit(solution)/shard_map/broadcast_in_dim | solution.py:399
  8.3 0.1 tile.12
  8.4 0.6 broadcast_in_dim.68.tags_ref
  9.0 1.5 %reshape.55.conv_w_ref = f32[8,1792]{1,0:T(8,128)} reshape(f32[2,4,1792]{2,1,0:T(4,128)} %param.22) | data formatting | bytes 114688 | tf_op jit(solution)/shard_map/reshape | solution.py:398
  10.5 1.1 %copy.16 = bf16[1536,24]{1,0:T(8,128)(2,1)S(1)} copy(bf16[1536,24]{0,1:T(8,128)(2,1)} %param.21) | data formatting | bytes 147456 | tf_op args[7]
  11.6 0.8 pad.11.dt_w_ref
  12.4 1.0 fusion.2.expand_ref
  13.4 0.0 copy-done
  13.4 85.6 %shard_map.136 = (bf16[256,1536]{1,0:T(8,128)(2,1)}, bf16[256,1536]{1,0:T(8,128)(2,1)}) custom-call(bf16[512,1536]{1,0:T(8,128)(2,1)} %tiles_ref.1, s32[1,512]{1,0:T(1,128)} %bitcast.6, f32[16,8,128]{2,1,0:T(8,128)} %broadcast_in_dim.68.tags_ref, bf16[1536,1536]{1,0:T(8,128)(2,1)} %slide_w_ref.1, f32[1,1536]{1,0:T(1,128)} %broadcast_in_dim.69.slide_b_ref, ...), custom_call_target="tpu_custom_call" | custom-call | flops 8000000000 | bytes 18000000 | tf_op jit(solution)/shard_map/pallas_call | solution.py:375
  99.0 5.1 %fusion = bf16[256,1536]{1,0:T(8,128)(2,1)} fusion(bf16[256,1536]{1,0:T(8,128)(2,1)} %get-tuple-element.8, bf16[1536,1536]{1,0:T(8,128)(2,1)} %param.27, bf16[256,1536]{1,0:T(8,128)(2,1)} %get-tuple-element.7), kind=kOutput, calls=%fused_computation.1 | convolution fusion | flops 1209139200 | bytes 7077888 | tf_op jit(solution)/shard_map/dot_general | solution.py:23
  (5 shorter events, 0.0 us)
Async XLA Ops:
  4.1 9.3 %copy-start = (s32[512]{0:T(512)}, s32[512]{0:T(512)S(1)}, u32[]{:S(2)}) copy-start(s32[512]{0:T(512)S(1)} %add_select_fusion.3) | copy-start | bytes 6148

commit v3 on v2

--- a/solution.py
+++ b/solution.py
@@ -52,9 +52,18 @@
     return jnp.dot(a, b, precision=precise, preferred_element_type=f32)
 
 
-def mixer_kernel(n, tiles_ref, target_ref, tags_ref, slide_w_ref, slide_b_ref, norm_ref, in_w_ref, dt_w_ref,
-                 conv_w_ref, conv_b_ref, dt_b_ref, a_log_ref, expand_ref, gain_ref, mixed_ref, embedded_ref,
-                 slide_w, in_w, out_rows, in_rows, in_tags, normed, gate_ref, cin_ref, dt_ref,
+def widen(values, expand):
+    high = values.astype(bf16).astype(f32)
+    rest = values - high
+    middle = rest.astype(bf16).astype(f32)
+    low = rest - middle
+    packed = high + pltpu.roll(middle, 32, 1) + pltpu.roll(low, 64, 1)
+    return dot(packed.astype(bf16), expand)
+
+
+def mixer_kernel(n, tiles_ref, target_ref, tags_ref, slide_w_ref, raw_slide_b_ref, raw_norm_ref, in_w_ref, dt_w_ref,
+                 conv_w_ref, conv_b_ref, raw_dt_b_ref, raw_a_log_ref, raw_gain_ref, out_w_ref, hidden_ref,
+                 mixed_ref, embedded_ref, slide_b_ref, norm_ref, gain_ref, dt_b_ref, a_log_ref, expand_ref, slide_w, in_w, out_rows, in_rows, in_tags, normed, gate_ref, cin_ref, dt_ref,
                  weight_sem, tag_send, tag_recv, row_send, row_recv, pad, halo, tots, totx, log_x, log_t, step_x, scaled, tail, write, read, acc, score,
                  sbuf, r1, tbuf, r2, pbuf, r3, halo_sem, tot_send, tot_recv, sem1s, sem1r, sem2s, sem2r, sem3s, sem3r):
     rows, e = gate_ref.shape
@@ -72,6 +81,18 @@
     barrier = pltpu.get_barrier_semaphore()
     for k in range(1, n):
         pl.semaphore_signal(barrier, inc=1, device_id={"seq": (me + k) % n}, device_id_type=pl.DeviceIdType.MESH)
+    slide_b_ref[...] = raw_slide_b_ref[...].reshape(1, e)
+    norm_ref[...] = raw_norm_ref[...].reshape(1, e)
+    gain_ref[...] = raw_gain_ref[...].reshape(1, e)
+    dt_b_ref[...] = jnp.zeros_like(dt_b_ref)
+    dt_b_ref[:, :HEADS] = raw_dt_b_ref[...]
+    a_log_ref[...] = jnp.zeros_like(a_log_ref)
+    a_log_ref[:, :HEADS] = raw_a_log_ref[...]
+    dt_ref[...] = jnp.zeros_like(dt_ref)
+    head_at = lax.broadcasted_iota(jnp.int32, (128, e), 0) % 32
+    lane_head = lax.broadcasted_iota(jnp.int32, (128, e), 1) // HEAD_DIM
+    third_at = lax.broadcasted_iota(jnp.int32, (128, e), 0)
+    expand_ref[...] = jnp.where((head_at == lane_head) & (third_at < 96), 1.0, 0.0).astype(bf16)
     weight_copies = [pltpu.make_async_copy(slide_w_ref, slide_w, weight_sem.at[0]),
                      pltpu.make_async_copy(in_w_ref, in_w, weight_sem.at[1])]
     for copy in weight_copies:
@@ -155,7 +176,9 @@
         return carry
 
     lax.fori_loop(0, e // 128, norm, 0)
-    dt_ref[...] = dot(normed[...], dt_w_ref[...])
+    dt_ref[:, :HEADS] = dot(normed[...], dt_w_ref[...])
+    out_copy = pltpu.make_async_copy(out_w_ref, slide_w, weight_sem.at[0])
+    out_copy.start()
     weight_copies[1].wait()
 
     def project_cin(c, carry):
@@ -183,6 +206,7 @@
     for d in range(2):
         x = dt_ref[...] + dt_b_ref[d:d + 1, :]
         step = jnp.maximum(x, 0.0) + jnp.log1p(jnp.exp(-jnp.abs(x)))
+        step = jnp.where(lax.broadcasted_iota(jnp.int32, step.shape, 1) < HEADS, step, 0.0)
         log_step = step * -jnp.exp(a_log_ref[d:d + 1, :])
         steps.append((step, log_step))
     own_tots = jnp.concatenate(
@@ -200,10 +224,9 @@
         reach = (t_at >= s_at) if d == 0 else (t_at <= s_at)
         log_decay = exact_dot(reach.astype(f32), log_step)
         log_t[d] = log_decay.T
-        log_x[d] = exact_dot(log_decay, expand_ref[...])
-        step_x[d] = exact_dot(step, expand_ref[...])
-
-    lax.fori_loop(0, e // 256, project_gate, 0)
+        log_x[d] = widen(log_decay, expand_ref[...])
+        step_x[d] = widen(step, expand_ref[...])
+
     for copy in halos:
         copy.wait()
 
@@ -220,7 +243,7 @@
         summed = conv_b_ref[d:d + 1, cols]
         for j in range(KERNEL):
             shift = j - (KERNEL - 1) if d == 0 else (KERNEL - 1) - j
-            taps = conv_w_ref[d * KERNEL + j:d * KERNEL + j + 1, cols]
+            taps = conv_w_ref[d, j:j + 1, cols]
             summed = summed + taps * pad[pl.ds(halo_width + shift, rows), cols]
         return summed * jax.nn.sigmoid(summed)
 
@@ -263,6 +286,8 @@
         for k in range(1, GROUP):
             first_copy(i, k).start()
         r1[i, q] = sbuf[i, q]
+
+    lax.fori_loop(0, e // 256, project_gate, 0)
 
     for d in range(2):
         reach = (t_at >= s_at) if d == 0 else (t_at <= s_at)
@@ -289,7 +314,7 @@
 
     for copy in tot_copies:
         copy.wait()
-    totx[...] = exact_dot(tots[...].reshape(n * 8, 128), expand_ref[...])
+    totx[...] = widen(tots[...].reshape(n * 8, 128), expand_ref[...])
     lax.fori_loop(0, 2, within, 0)
 
     def lanes_of(i):
@@ -356,17 +381,23 @@
         return carry
 
     lax.fori_loop(0, e // 128, emit, 0)
+    out_copy.wait()
+
+    def final(c, carry):
+        cols = pl.ds(pl.multiple_of(c * 256, 256), 256)
+        hidden_ref[:, cols] = (embedded_ref[:, cols].astype(f32) + dot(mixed_ref[...], slide_w[:, cols])).astype(bf16)
+        return carry
+
+    lax.fori_loop(0, e // 256, final, 0)
 
 
 def layer(devices, tile_embeds, target, tags, slide_weight, slide_bias, norm_gain, in_weight, dt_weight,
-          conv_weight, conv_bias, dt_bias, a_log, out_gain):
+          conv_weight, conv_bias, dt_bias, a_log, out_gain, out_weight):
     slots, e = tile_embeds.shape
     rows = slots // 2
     wide = e + 2 * NS
     pieces = e // GROUP // 128
     planes = devices // GROUP
-    pad_heads = ((0, 0), (0, 128 - HEADS))
-    expand = (jnp.arange(128)[:, None] == (jnp.arange(e) // HEAD_DIM)[None, :]).astype(f32)
     dma = pltpu.SemaphoreType.DMA
     vmem = pltpu.VMEM
     held = pl.BlockSpec(memory_space=pltpu.VMEM)
@@ -374,10 +405,12 @@
     loads = e // LOAD
     return pl.pallas_call(
         functools.partial(mixer_kernel, devices),
-        out_shape=[jax.ShapeDtypeStruct((rows, e), bf16), jax.ShapeDtypeStruct((rows, e), bf16)],
-        in_specs=[held, held, held, far, held, held, far] + [held] * 7,
-        out_specs=[held, held],
+        out_shape=jax.ShapeDtypeStruct((rows, e), bf16),
+        in_specs=[held, held, held, far, held, held, far] + [held] * 6 + [far],
+        out_specs=held,
         scratch_shapes=[
+            vmem((rows, e), bf16), vmem((rows, e), bf16), vmem((1, e), f32), vmem((1, e), f32), vmem((1, e), f32),
+            vmem((2, 128), f32), vmem((2, 128), f32), vmem((128, e), bf16),
             vmem((e, e), bf16), vmem((e, e + wide), bf16), vmem((loads, slots, LOAD), bf16),
             vmem((loads, slots, LOAD), bf16), vmem((devices, 8, 128), f32), vmem((rows, e), bf16),
             vmem((rows, e), bf16), vmem((rows, wide), bf16), vmem((rows, 128), f32),
@@ -394,9 +427,8 @@
         ],
         compiler_params=pltpu.CompilerParams(collective_id=0, has_side_effects=True, vmem_limit_bytes=58 * 2**20),
         cost_estimate=pl.CostEstimate(flops=8 * 10**9, bytes_accessed=18 * 10**6, transcendentals=4 * 10**6),
-    )(tile_embeds, target, tags, slide_weight, slide_bias[None], norm_gain[None], in_weight,
-      jnp.pad(dt_weight, pad_heads), conv_weight.reshape(2 * KERNEL, wide), conv_bias, jnp.pad(dt_bias, pad_heads),
-      jnp.pad(a_log, pad_heads), expand, out_gain[None])
+    )(tile_embeds, target, tags, slide_weight, slide_bias, norm_gain, in_weight, dt_weight, conv_weight, conv_bias,
+      dt_bias, a_log, out_gain, out_weight)
 
 
 def per_device(tile_embeds, tile_pos, tile_count, slide_weight, slide_bias, norm_gain, in_weight,
@@ -404,9 +436,8 @@
     devices = lax.axis_size("seq")
     rows = tile_embeds.shape[0] // 2
     target, tags = plan(tile_pos, tile_count, devices, rows)
-    mixed, embedded = layer(devices, tile_embeds, target, tags, slide_weight, slide_bias, norm_gain, in_weight,
-                            dt_weight, conv_weight, conv_bias, dt_bias, a_log, out_gain)
-    return (embedded.astype(f32) + dot(mixed, out_weight)).astype(bf16)
+    return layer(devices, tile_embeds, target, tags, slide_weight, slide_bias, norm_gain, in_weight,
+                 dt_weight, conv_weight, conv_bias, dt_bias, a_log, out_gain, out_weight)
 
 
 def solution(mesh):

time: 105 us -> 91.4 us (0.87)
  local copies, waits for them, and re-layouts: 10.6 us -> 4.67 us
  matrix products: 5.32 us -> 0.27 us
  Pallas kernels: 85.6 us -> 84.5 us
    dot_general x2 -> x1, matrix products: 5.32 us -> 0.27 us  [dot(): return jnp.dot(a, b, preferred_element_type=f32)]
    broadcast_in_dim x3 -> x0, local copies, waits for them, and re-layouts: 3.88 us -> none  [the longest x1 1.3 us: layer(): slide_bias[None]]
    pad x3 -> x0, local copies, waits for them, and re-layouts: 3.31 us -> none  [the longest x1 1.25 us: layer(): jnp.pad(dt_bias, pad_heads)]
    unnamed x3 -> x4, local copies, waits for them, and re-layouts: 1.11 us -> 3.87 us
    reshape x1 -> x0, local copies, waits for them, and re-layouts: 1.46 us -> none  [layer(): conv_weight.reshape(2 * KERNEL, wide)]
where the time goes in v3:
time: 91.4 us; the launch traced here: 91.1 us
  Pallas kernels  84.5 us (92%)
  local copies, waits for them, and re-layouts  4.67 us (5%)
    pallas_call x1, Pallas kernels, layer(): pl.pallas_call(functools.partial(mixer_kernel, devices), out_shape=jax.Sh...  84.5 us
    unnamed x4, local copies, waits for them, and re-layouts  3.87 us

profile of v3, /device:TPU:0, one launch (start us, length us, event | category | flops | bytes accessed | tf_op | source)
XLA Modules:
  0.0 91.1 jit_solution(16941591263600484035)
XLA Ops:
  0.7 0.7 fusion.4
  1.4 0.3 fusion
  1.6 0.0 copy-start
  1.7 0.2 select_reduce_fusion
  1.8 0.1 tile.10
  1.9 0.1 tile.12
  2.0 0.6 broadcast_in_dim.57.tags_ref
  2.7 1.8 %copy.16.dt_w_ref = bf16[1536,24]{1,0:T(8,128)(2,1)} copy(bf16[1536,24]{0,1:T(8,128)(2,1)} %param.21) | data formatting | bytes 147456 | tf_op args[7]
  4.5 0.0 copy-done
  4.5 84.5 %shard_map.136 = bf16[256,1536]{1,0:T(8,128)(2,1)} custom-call(bf16[512,1536]{1,0:T(8,128)(2,1)} %tiles_ref.1, s32[1,512]{1,0:T(1,128)} %bitcast.4, f32[16,8,128]{2,1,0:T(8,128)} %broadcast_in_dim.57.tags_ref, bf16[1536,1536]{1,0:T(8,128)(2,1)} %slide_w_ref.1, f32[1536]{0:T(1024)} %raw_slide_b_ref.1, f32[1536]{0:T(1024)} %raw_norm_ref.1, ...), custom_call_target="tpu_custom_call" | custom-call | flops 8000000000 | bytes 18000000 | tf_op jit(solution)/shard_map/pallas_call | solution.py:406
  89.0 2.1 %copy.19 = bf16[256,1536]{1,0:T(8,128)(2,1)} copy(bf16[256,1536]{1,0:T(8,128)(2,1)} %shard_map.136) | data formatting | bytes 1572864
  (4 shorter events, 0.0 us)
Async XLA Ops:
  1.6 2.8 %copy-start = (s32[512]{0:T(512)}, s32[512]{0:T(512)S(1)}, u32[]{:S(2)}) copy-start(s32[512]{0:T(512)S(1)} %add_select_fusion.2) | copy-start | bytes 6148
